TPU v7x, 32 devices: a whole 2x2x4 slice. The times are simulated.
32 devices in a mesh: groups: 2 (over y), mp: 16 (over z, x, core).
Axes of the slice: x: 2, y: 2, z: 4, core: 2. Of those that a mesh axis runs over, the one named last changes fastest.
Arguments:
- residual: bfloat16 [256, 8192], P(('groups', 'mp')), parts along dimension 0, may hold values from -6 to 6
- prenorm_scale: float32 [8192], replicated, may hold values from 0.1 to 1.9
- gate_weight_matrix: bfloat16 [8192, 28672], P(None, 'mp'), may hold values from -0.0625 to 0.0625
- up_weight_matrix: bfloat16 [8192, 28672], P(None, 'mp'), may hold values from -0.0625 to 0.0625
- down_factor_weight: bfloat16 [32, 32, 8192], P('mp'), may hold values from -0.0625 to 0.0625
- up_factor_weight: bfloat16 [32, 32, 28672], P(None, None, 'mp'), may hold values from -1 to 1
- token_adapter_ids: int32 [256, 1], P('groups'), parts along dimension 0, may hold values from 0 to 31; in each aligned block of 128 rows (0 to 127, 128 to 255, ...) at most 8 rows name the same one
- adapter_store_rows: int32 [32], replicated, may hold values from 0 to 31, each once
Outputs:
- hidden: bfloat16 [256, 28672], P('groups', 'mp'), parts along dimension 0
There are 2 independent parts, one for each index of `groups`. A program takes and returns all parts, laid end to end along the dimension named above; an argument that names none is the same for every part. Nothing has to cross between parts.
Inputs may be any that keep to these rules, and one draw needn't show every extreme that they name: `token_adapter_ids`: each adapter is named by at most 8 tokens of a replica, a bound that some block reaches. Each value appears once: adapter a's factors are row adapter_store_rows[a] of down_factor_weight and up_factor_weight.
All inputs are finite; a program needn't handle non-finite values.
Results may differ from a plain program's by a relative error of at most 0.0066.
Values may be sent and summed in bfloat16 or wider, within the bound.
A program may use at most 192 MiB of HBM per device.

v0:
```python
import jax
import jax.numpy as jnp
from jax import lax
from jax.sharding import PartitionSpec as P

SEGMENT_SLOTS = 8


ADAPTER_SCALE = 2.0


def slot_rows(token_adapter_ids, adapter_store_rows, capacity):
    slot_ids = adapter_store_rows[token_adapter_ids[:, 0]]
    adapter_list = adapter_store_rows.shape[0]
    onehot = (slot_ids[:, None] == jnp.arange(adapter_list, dtype=jnp.int32)[None, :]).astype(
        jnp.int32
    )
    earlier = jnp.cumsum(onehot, axis=0) - onehot
    within = jnp.sum(earlier * onehot, axis=1)
    return slot_ids * capacity + within


def on_device(
    residual,
    prenorm_scale,
    gate_weight_matrix,
    up_weight_matrix,
    down_factor_weight,
    up_factor_weight,
    token_adapter_ids,
    adapter_store_rows,
):
    widened = residual.astype(jnp.float32)
    rescale = lax.rsqrt(jnp.mean(widened * widened, axis=1, keepdims=True) + 1e-05)
    normalized_input = (widened * rescale * prenorm_scale).astype(jnp.bfloat16)
    store_row_index = slot_rows(token_adapter_ids, adapter_store_rows, SEGMENT_SLOTS)
    adapter_list = adapter_store_rows.shape[0]
    local_slot_rows = down_factor_weight.shape[0]
    reduced_width = down_factor_weight.shape[1]
    adapter_rank_size = reduced_width // 2
    hidden_model_width = down_factor_weight.shape[2]
    output_columns = gate_weight_matrix.shape[1]
    held_rows = local_slot_rows * SEGMENT_SLOTS
    targets = lax.axis_index("mp") * held_rows + jnp.arange(held_rows, dtype=jnp.int32)
    chooser = (store_row_index[None, :] == targets[:, None]).astype(jnp.bfloat16)
    gathered = lax.all_gather(normalized_input, "mp", axis=0, tiled=True)
    plain_gate_output = jnp.dot(gathered, gate_weight_matrix, preferred_element_type=jnp.float32)
    plain_up_output = jnp.dot(gathered, up_weight_matrix, preferred_element_type=jnp.float32)
    selected_factors = jnp.dot(chooser, gathered, preferred_element_type=jnp.float32).astype(
        jnp.bfloat16
    )
    reduced_tokens = jnp.einsum(
        "unr,ugr->ung",
        selected_factors.reshape(local_slot_rows, SEGMENT_SLOTS, hidden_model_width),
        down_factor_weight,
        preferred_element_type=jnp.float32,
    ).astype(jnp.bfloat16)
    flat_shrunk = reduced_tokens.reshape(held_rows * reduced_width)
    all_tokens_group = lax.all_gather(flat_shrunk, "mp", axis=0, tiled=True).reshape(
        adapter_list * SEGMENT_SLOTS, reduced_width
    )
    reduced_pair_rows = all_tokens_group.reshape(adapter_list, SEGMENT_SLOTS, 2, adapter_rank_size)
    adapter_factors = up_factor_weight.reshape(adapter_list, 2, adapter_rank_size, output_columns)
    adapter_correction = jnp.einsum(
        "jyon,jonq->ojyq", reduced_pair_rows, adapter_factors, preferred_element_type=jnp.float32
    ).reshape(2, adapter_list * SEGMENT_SLOTS, output_columns)
    gate_total_output = plain_gate_output + ADAPTER_SCALE * adapter_correction[0][store_row_index]
    up_total_output = plain_up_output + ADAPTER_SCALE * adapter_correction[1][store_row_index]
    return (jax.nn.silu(gate_total_output) * up_total_output).astype(jnp.bfloat16)


def solution(mesh):
    in_specs = (
        P(("groups", "mp"), None),
        P(),
        P(None, "mp"),
        P(None, "mp"),
        P("mp", None, None),
        P(None, None, "mp"),
        P("groups", None),
        P(),
    )
    out_specs = P("groups", "mp")
    return jax.shard_map(
        on_device, mesh=mesh, in_specs=in_specs, out_specs=out_specs, check_vma=False
    )
```

profile of v0, /device:TPU:0, one launch (start us, length us, event | category | flops | bytes accessed | tf_op | source)
XLA Modules:
  0.0 120.5 jit_solution(8317825637239976106)
XLA Ops:
  6.5 0.0 copy-start
  6.5 0.0 all-gather.3.cloned.1.call-start
  6.5 1.2 fusion.5
  7.7 1.7 %fusion.7 = bf16[8,8192]{1,0:T(8,128)(2,1)} fusion(bf16[8,8192]{1,0:T(8,128)(2,1)} %param.8, f32[8192]{0:T(1024)} %param.9, f32[8]{0:T(128)S(1)} %add_rsqrt_fusion), kind=kLoop, calls=%fused_computation.18 | loop fusion | flops 262144 | bytes 294944 | tf_op jit(solution)/shard_map/convert_element_type | solution.py:35
  9.4 0.0 all-gather.3.cloned.1.call-update
  9.4 0.7 fusion.16
  10.1 1.6 %gather_fusion = s32[128]{0:T(128)S(1)} fusion(s32[32]{0:T(128)} %param.15, s32[1024]{0:T(1024)S(1)} %pad_clamp_fusion.1), kind=kCustom, calls=%fused_computation | custom fusion | bytes 1536 | tf_op jit(solution)/shard_map/gather | solution.py:13
  11.7 0.1 fusion.9
  11.8 0.2 reduce_window_sum.11
  11.9 0.2 select_reduce_fusion
  12.1 41.5 %all-gather.3.cloned.1.call-done = bf16[128,8192]{1,0:T(8,128)(2,1)} async-done(((bf16[8,8192]{1,0:T(8,128)(2,1)}), bf16[128,8192]{1,0:T(8,128)(2,1)}) %all-gather.3.cloned.1.call-update) | async-done | bytes 2097168 | tf_op jit(solution)/shard_map/all_gather | solution.py:46
  53.7 0.0 copy-done
  53.7 2.3 %convolution_convert_fusion.1 = bf16[2,8,32]{2,1,0:T(8,128)(2,1)S(1)} fusion(bf16[2,32,8192]{2,1,0:T(8,128)(2,1)S(1)} %copy-done, bf16[128,8192]{1,0:T(8,128)(2,1)} %all-gather.3.cloned.1.call-done, s32[128]{0:T(128)S(1)} %get-tuple-element.6, s32[16]{0:T(128)S(1)} %iota_add_fusion), kind=kOutput, calls=%fused_computation.13 | convolution fusion | flops 42076672 | bytes 3147328 | tf_op jit(solution)/shard_map/unr,ugr->ung/dot_general | solution.py:52
  56.0 0.1 reshape.87
  56.0 19.3 %all-gather = bf16[16,1,512]{2,1,0:T(2,128)(2,1)S(1)} all-gather(bf16[1,1,512]{2,1,0:T(2,128)(2,1)S(1)} %reshape.87), channel_id=1, replica_groups=mesh['groups'=2,'mp'=16] {'mp'}, dimensions={0}, use_global_device_ids=true | all-gather | bytes 17408 | tf_op jit(solution)/shard_map/all_gather | solution.py:59
  75.3 0.1 reduce
  75.4 0.1 reshape_reshape.3
  75.6 2.7 %fusion.1 = f32[2,32,8,1792]{3,2,1,0:T(8,128)S(1)} fusion(bf16[32,2,16,1792]{3,2,1,0:T(8,128)(2,1)} %bitcast.21, bf16[32,8,2,16]{3,2,1,0:T(2,128)(2,1)S(1)} %reshape_reshape.3), kind=kOutput, calls=%fused_computation.5 | convolution fusion | flops 29360128 | bytes 7356416 | tf_op jit(solution)/shard_map/jyon,jonq->ojyq/dot_general | solution.py:64
  78.2 1.5 %slice_bitcast_fusion.1 = (f32[256,1792]{1,0:T(8,128)}, f32[256,1792]{1,0:T(8,128)S(1)}) fusion(f32[2,32,8,1792]{3,2,1,0:T(8,128)S(1)} %fusion.1), kind=kLoop, calls=%fused_computation.12 | loop fusion | bytes 7340032 | tf_op jit(solution)/shard_map/squeeze | solution.py:67
  79.7 2.8 %gather_fusion.1 = f32[128,1792]{1,0:T(8,128)S(1)} fusion(f32[256,1792]{1,0:T(8,128)} %get-tuple-element.7, s32[1024]{0:T(1024)S(1)} %pad_clamp_fusion), kind=kCustom, calls=%fused_computation.1 | custom fusion | bytes 1835520 | tf_op jit(solution)/shard_map/gather | solution.py:67
  82.5 1.9 %gather_fusion.2 = f32[128,1792]{1,0:T(8,128)} fusion(f32[256,1792]{1,0:T(8,128)S(1)} %get-tuple-element.8, s32[1024]{0:T(1024)S(1)} %pad_clamp_fusion), kind=kCustom, calls=%fused_computation.2 | custom fusion | bytes 1835520 | tf_op jit(solution)/shard_map/gather | solution.py:68
  84.4 0.0 copy-start.2
  84.4 0.0 copy-start.3
  84.4 14.7 %convolution_add_fusion.1 = f32[128,1792]{1,0:T(8,128)S(1)} fusion(bf16[128,8192]{1,0:T(8,128)(2,1)} %all-gather.3.cloned.1.call-done, bf16[8192,1792]{1,0:T(8,128)(2,1)} %param.10, f32[128,1792]{1,0:T(8,128)S(1)} %gather_fusion.1), kind=kOutput, calls=%fused_computation.9 | convolution fusion | flops 3758555136 | bytes 33292288 | tf_op jit(solution)/shard_map/dot_general | solution.py:47
  99.2 0.0 copy-done.2
  99.2 0.0 copy-done.3
  99.2 0.0 copy-start.1
  99.2 14.4 %fusion.4 = bf16[128,1792]{1,0:T(8,128)(2,1)} fusion(bf16[128,8192]{1,0:T(8,128)(2,1)S(1)} %copy-done.2, bf16[8192,1792]{1,0:T(8,128)(2,1)} %param.11, f32[128,1792]{1,0:T(8,128)S(1)} %copy-done.3, f32[128,1792]{1,0:T(8,128)S(1)} %convolution_add_fusion.1), kind=kOutput, calls=%fused_computation.10 | convolution fusion | flops 3759931392 | bytes 33751040 | tf_op jit(solution)/shard_map/dot_general | solution.py:48
  113.6 0.0 copy-done.1
  (5 shorter events, 0.0 us)
Async XLA Ops:
  6.5 47.1 %copy-start = (bf16[2,32,8192]{2,1,0:T(8,128)(2,1)S(1)}, bf16[2,32,8192]{2,1,0:T(8,128)(2,1)}, u32[]{:S(2)}) copy-start(bf16[2,32,8192]{2,1,0:T(8,128)(2,1)} %param.12) | copy-start | bytes 3145732
  6.5 47.1 %all-gather.3.cloned.1.call-start = ((), (), s32[]{:S(2)}) async-start(), calls=%async_computation | async-start | bytes 2228224 | tf_op jit(solution)/shard_map/all_gather | solution.py:46
  84.4 14.8 %copy-start.2 = (bf16[128,8192]{1,0:T(8,128)(2,1)S(1)}, bf16[128,8192]{1,0:T(8,128)(2,1)}, u32[]{:S(2)}) copy-start(bf16[128,8192]{1,0:T(8,128)(2,1)} %all-gather.3.cloned.1.call-done) | copy-start | bytes 6291460
  84.4 14.8 %copy-start.3 = (f32[128,1792]{1,0:T(8,128)S(1)}, f32[128,1792]{1,0:T(8,128)}, u32[]{:S(2)}) copy-start(f32[128,1792]{1,0:T(8,128)} %gather_fusion.2) | copy-start | bytes 2752516
  99.2 14.4 %copy-start.1 = (bf16[2,32,8192]{2,1,0:T(8,128)(2,1)S(1)}, bf16[2,32,8192]{2,1,0:T(8,128)(2,1)}, u32[]{:S(2)}) copy-start(bf16[2,32,8192]{2,1,0:T(8,128)(2,1)} %param.12) | copy-start | bytes 3145732
Sparse Core Ops, SparseCore 0:
  9.5 44.0 all-gather.2
where the time goes:
time: 121 us; the launch traced here: 120 us
  waiting for transfers between devices  41.5 us (34%)
  matrix products  34.1 us (28%)
  blocking collectives  19.3 us (16%)
  between operations  13.5 us (11%)
  local copies, waits for them, and re-layouts  8.05 us (7%)
  other arithmetic  4.05 us (3%)
    all_gather x1, waiting for transfers between devices, on_device(): gathered = lax.all_gather(normalized_input, 'mp', axis=0, tiled=True)  41.5 us
    all_gather x1, blocking collectives, on_device(): lax.all_gather(flat_shrunk, 'mp', axis=0, tiled=True)  19.3 us
    dot_general x1, matrix products, on_device(): jnp.dot(gathered, gate_weight_matrix, preferred_element_type=jnp.float32)  14.7 us
    dot_general x1, matrix products, on_device(): jnp.dot(gathered, up_weight_matrix, preferred_element_type=jnp.float32)  14.4 us
    gather x1, local copies, waits for them, and re-layouts, on_device(): adapter_correction[0][store_row_index]  2.84 us
    dot_general x1, matrix products, on_device(): jnp.einsum('jyon,jonq->ojyq', reduced_pair_rows, adapter_factors, preferr...  2.66 us
  transfers between devices with their start and end apart: 1, of which 1 were waited for; matrix products, arithmetic and copies ran while one was open for 2% of the time, Pallas kernels for 0%

commit v1 on v0

--- a/solution.py
+++ b/solution.py
@@ -1,9 +1,16 @@
 import jax
 import jax.numpy as jnp
 from jax import lax
+from jax.experimental import pallas as pl
+from jax.experimental.pallas import tpu as pltpu
 from jax.sharding import PartitionSpec as P
 
 SEGMENT_SLOTS = 8
+CHUNK = 1024
+WIDE = 256
+LINES = 4
+LANES = 4
+MESH = pl.DeviceIdType.MESH
 
 
 ADAPTER_SCALE = 2.0
@@ -69,6 +76,412 @@
     return (jax.nn.silu(gate_total_output) * up_total_output).astype(jnp.bfloat16)
 
 
+def supported(mesh, model, columns, adapters, tokens, rows, width):
+    members = mesh.shape["mp"]
+    return (
+        members == LINES * LANES
+        and tokens == members * rows
+        and tokens == 128
+        and rows == 8
+        and model % CHUNK == 0
+        and model // CHUNK >= 4
+        and columns % 256 == 0
+        and columns <= 2048
+        and adapters == 2 * members
+        and width == 32
+    )
+
+
+def fused_kernel(
+    residual_hbm,
+    scale_hbm,
+    gate_hbm,
+    up_hbm,
+    down_hbm,
+    factor_hbm,
+    ids_hbm,
+    rows_hbm,
+    out_ref,
+    residual,
+    scale,
+    ids,
+    store_rows,
+    down,
+    factor,
+    blocks,
+    features,
+    gate_ring,
+    up_ring,
+    gate_total,
+    up_total,
+    shrunk_total,
+    shrunk_all,
+    small_sem,
+    down_sem,
+    factor_sem,
+    gate_sem,
+    up_sem,
+    z_send,
+    z_recv,
+    x_send,
+    x_recv,
+    c_send,
+    c_recv,
+    s_send,
+    s_recv,
+):
+    members = LINES * LANES
+    me = lax.axis_index("mp")
+    z = me // 4
+    x = (me // 2) % 2
+    c = me % 2
+    model = residual.shape[1]
+    chunks = model // CHUNK
+    half = CHUNK // 2
+    columns = gate_hbm.shape[1]
+    slots = gate_ring.shape[0]
+    adapters = factor.shape[0]
+    tokens = members * SEGMENT_SLOTS
+    slot_total = adapters * SEGMENT_SLOTS
+    f32, bf16 = jnp.float32, jnp.bfloat16
+
+    def rows_of(i):
+        return pl.ds(pl.multiple_of(i * CHUNK, CHUNK), CHUNK)
+
+    def gate_copy(i):
+        s = lax.rem(i, slots)
+        return pltpu.make_async_copy(gate_hbm.at[rows_of(i)], gate_ring.at[s], gate_sem.at[s])
+
+    def up_copy(i):
+        s = lax.rem(i, slots)
+        return pltpu.make_async_copy(up_hbm.at[rows_of(i)], up_ring.at[s], up_sem.at[s])
+
+    small = [
+        pltpu.make_async_copy(source, target, small_sem.at[k])
+        for k, (source, target) in enumerate(
+            ((residual_hbm, residual), (scale_hbm, scale), (ids_hbm, ids), (rows_hbm, store_rows))
+        )
+    ]
+    for copy in small:
+        copy.start()
+    down_copy = pltpu.make_async_copy(down_hbm, down, down_sem)
+    down_copy.start()
+    factor_copy = pltpu.make_async_copy(factor_hbm, factor, factor_sem)
+
+    barrier = pltpu.get_barrier_semaphore()
+
+    @pl.loop(1, members)
+    def _(k):
+        pl.semaphore_signal(
+            barrier, inc=1, device_id={"mp": lax.rem(me + k, members)}, device_id_type=MESH
+        )
+
+    @pl.loop(0, slots)
+    def _(i):
+        gate_copy(i).start()
+        up_copy(i).start()
+
+    factor_copy.start()
+
+    small[0].wait()
+    small[1].wait()
+    wide = residual[...].astype(f32)
+    rescale = lax.rsqrt(jnp.mean(wide * wide, axis=1, keepdims=True) + 1e-05)
+    for i in range(chunks):
+        first = slice(i * CHUNK, i * CHUNK + half)
+        second = slice(i * CHUNK + half, (i + 1) * CHUNK)
+        top = residual[:, first].astype(f32) * rescale * scale[:, first]
+        bottom = residual[:, second].astype(f32) * rescale * scale[:, second]
+        blocks[i, z, x, c] = jnp.concatenate([top, bottom], axis=0).astype(bf16)
+
+    pl.semaphore_wait(barrier, members - 1)
+
+    def z_copy(i, k):
+        other = lax.rem(z + k, LINES)
+        return pltpu.make_async_remote_copy(
+            src_ref=blocks.at[i, z, x, c],
+            dst_ref=blocks.at[i, z, x, c],
+            send_sem=z_send.at[i, other],
+            recv_sem=z_recv.at[i, z],
+            device_id={"mp": other * LANES + x * 2 + c},
+            device_id_type=MESH,
+        )
+
+    def z_arrival(i, k):
+        other = lax.rem(z + k, LINES)
+        return pltpu.make_async_remote_copy(
+            src_ref=blocks.at[i, other, x, c],
+            dst_ref=blocks.at[i, other, x, c],
+            send_sem=z_send.at[i, other],
+            recv_sem=z_recv.at[i, other],
+            device_id={"mp": other * LANES + x * 2 + c},
+            device_id_type=MESH,
+        )
+
+    def x_copy(i, lane):
+        return pltpu.make_async_remote_copy(
+            src_ref=blocks.at[i, :, lane, c],
+            dst_ref=blocks.at[i, :, lane, c],
+            send_sem=x_send.at[i],
+            recv_sem=x_recv.at[i],
+            device_id={"mp": z * LANES + (1 - x) * 2 + c},
+            device_id_type=MESH,
+        )
+
+    def c_copy(i, core):
+        return pltpu.make_async_remote_copy(
+            src_ref=blocks.at[i, :, :, core],
+            dst_ref=blocks.at[i, :, :, core],
+            send_sem=c_send.at[i],
+            recv_sem=c_recv.at[i],
+            device_id={"mp": z * LANES + x * 2 + (1 - c)},
+            device_id_type=MESH,
+        )
+
+    def s_copy(k):
+        other = lax.rem(me + k, members)
+        return pltpu.make_async_remote_copy(
+            src_ref=shrunk_all.at[me],
+            dst_ref=shrunk_all.at[me],
+            send_sem=s_send.at[other],
+            recv_sem=s_recv.at[me],
+            device_id={"mp": other},
+            device_id_type=MESH,
+        )
+
+    def s_arrival(k):
+        other = lax.rem(me + k, members)
+        return pltpu.make_async_remote_copy(
+            src_ref=shrunk_all.at[other],
+            dst_ref=shrunk_all.at[other],
+            send_sem=s_send.at[other],
+            recv_sem=s_recv.at[other],
+            device_id={"mp": other},
+            device_id_type=MESH,
+        )
+
+    @pl.loop(0, chunks)
+    def _(i):
+        for k in range(1, LINES):
+            z_copy(i, k).start()
+
+    gate_total[...] = jnp.zeros_like(gate_total)
+    up_total[...] = jnp.zeros_like(up_total)
+    shrunk_total[...] = jnp.zeros_like(shrunk_total)
+    small[2].wait()
+    small[3].wait()
+    down_copy.wait()
+
+    named = (lax.broadcasted_iota(jnp.int32, (adapters, tokens), 0) == ids[...]).astype(f32)
+    stored = (lax.broadcasted_iota(jnp.int32, (adapters, adapters), 0) == store_rows[...]).astype(f32)
+    in_slot = jnp.dot(stored.astype(bf16), named.astype(bf16), preferred_element_type=f32)
+    before = (
+        lax.broadcasted_iota(jnp.int32, (tokens, tokens), 0)
+        < lax.broadcasted_iota(jnp.int32, (tokens, tokens), 1)
+    ).astype(f32)
+    earlier = jnp.dot(in_slot.astype(bf16), before.astype(bf16), preferred_element_type=f32)
+    slot_number = lax.broadcasted_iota(jnp.int32, (adapters, tokens), 0).astype(f32)
+    slot_row = jnp.sum(in_slot * (earlier + SEGMENT_SLOTS * slot_number), axis=0, keepdims=True)
+
+    def gather_step(g):
+        @pl.when(g < chunks)
+        def _():
+            for k in range(1, LINES):
+                z_arrival(g, k).wait_recv()
+            x_copy(g, x).start()
+
+        @pl.when((g >= 1) & (g <= chunks))
+        def _():
+            x_copy(g - 1, 1 - x).wait_recv()
+            c_copy(g - 1, c).start()
+
+        @pl.when((g >= 2) & (g <= chunks + 1))
+        def _():
+            i = g - 2
+            c_copy(i, 1 - c).wait_recv()
+            taken = blocks[i].reshape(members, 16, half).astype(f32)
+            for h in range(2):
+                part = taken[:, h * 8 : (h + 1) * 8, :].reshape(tokens, half).astype(bf16)
+                features[i, :, h * half : (h + 1) * half] = part
+            factors = down[:, :, rows_of(i)].reshape(-1, CHUNK)
+            shrunk_total[...] += lax.dot_general(
+                features[i], factors, (((1,), (1,)), ((), ())), preferred_element_type=f32
+            )
+
+    def multiply(total, left, right_of):
+        for j in range(columns // WIDE):
+            cut = slice(j * WIDE, (j + 1) * WIDE)
+            total[:, cut] += jnp.dot(left, right_of(cut), preferred_element_type=f32)
+
+    def gate_step(i):
+        gate_copy(i).wait()
+        s = lax.rem(i, slots)
+        multiply(gate_total, features[i], lambda cut: gate_ring[s, :, cut])
+
+        @pl.when(i + slots < chunks)
+        def _():
+            gate_copy(i + slots).start()
+
+    def up_step(i):
+        up_copy(i).wait()
+        s = lax.rem(i, slots)
+        multiply(up_total, features[i], lambda cut: up_ring[s, :, cut])
+
+        @pl.when(i + slots < chunks)
+        def _():
+            up_copy(i + slots).start()
+
+    for g in range(3):
+        gather_step(g)
+
+    @pl.loop(0, chunks - 3)
+    def _(i):
+        gate_step(i)
+        gather_step(3 + i + (i + 1) // 2)
+        up_step(i)
+
+        @pl.when(i % 2 == 0)
+        def _():
+            gather_step(4 + i + (i + 1) // 2)
+
+    wanted = (me * 16 + lax.broadcasted_iota(jnp.int32, (16, tokens), 0)).astype(f32)
+    chooser = (slot_row == wanted).astype(f32).astype(bf16)
+    rounded = shrunk_total[...].astype(bf16)
+    mine = jnp.dot(chooser, rounded, preferred_element_type=f32)
+    row = lax.broadcasted_iota(jnp.int32, mine.shape, 0)
+    lane = lax.broadcasted_iota(jnp.int32, mine.shape, 1)
+    mine = jnp.where((row < 8) == (lane < 32), mine, 0.0)
+    shrunk_all[me] = jnp.concatenate([mine, jnp.zeros_like(mine)], axis=1).astype(bf16)
+
+    @pl.loop(1, members)
+    def _(k):
+        s_copy(k).start()
+
+    @pl.loop(chunks - 3, chunks - 1)
+    def _(i):
+        gate_step(i)
+        up_step(i)
+
+    @pl.loop(1, members)
+    def _(k):
+        s_arrival(k).wait_recv()
+
+    token_of = (
+        lax.broadcasted_iota(jnp.int32, (slot_total, tokens), 0).astype(f32) == slot_row
+    ).astype(f32)
+    row_of = jnp.transpose(token_of).astype(bf16)
+    gathered = shrunk_all[...].reshape(slot_total, 128)
+    factor_copy.wait()
+    spread_shape = (128, adapters * 16)
+    for p, total in enumerate((gate_total, up_total)):
+        lane = lax.broadcasted_iota(jnp.int32, spread_shape, 0)
+        place = lax.broadcasted_iota(jnp.int32, spread_shape, 1)
+        spreader = ((lane % 32 == p * 16 + place % 16) & (lane < 64)).astype(f32).astype(bf16)
+        spread = jnp.dot(gathered, spreader, preferred_element_type=f32)
+        owner = lax.broadcasted_iota(jnp.int32, spread.shape, 0) // SEGMENT_SLOTS
+        place = lax.broadcasted_iota(jnp.int32, spread.shape, 1) // 16
+        spread = jnp.where(owner == place, spread * ADAPTER_SCALE, 0.0).astype(bf16)
+        left = jnp.dot(row_of, spread, preferred_element_type=f32).astype(bf16)
+        multiply(
+            total,
+            left,
+            lambda cut, p=p: factor[:, p * 16 : (p + 1) * 16, cut].reshape(adapters * 16, WIDE),
+        )
+
+    gate_step(chunks - 1)
+    up_step(chunks - 1)
+    for j in range(columns // WIDE):
+        cut = slice(j * WIDE, (j + 1) * WIDE)
+        value = gate_total[:, cut]
+        out_ref[:, cut] = (value / (1.0 + jnp.exp(-value)) * up_total[:, cut]).astype(bf16)
+
+    @pl.loop(0, chunks)
+    def _(i):
+        for k in range(1, LINES):
+            z_copy(i, k).wait_send()
+        x_copy(i, x).wait_send()
+        c_copy(i, c).wait_send()
+
+    @pl.loop(1, members)
+    def _(k):
+        s_copy(k).wait_send()
+
+
+def fused(
+    residual,
+    prenorm_scale,
+    gate_weight_matrix,
+    up_weight_matrix,
+    down_factor_weight,
+    up_factor_weight,
+    token_adapter_ids,
+    adapter_store_rows,
+):
+    rows, model = residual.shape
+    columns = gate_weight_matrix.shape[1]
+    tokens = token_adapter_ids.shape[0]
+    adapters = adapter_store_rows.shape[0]
+    members = LINES * LANES
+    chunks = model // CHUNK
+    slots = min(6, chunks)
+    half = CHUNK // 2
+    bf16, f32 = jnp.bfloat16, jnp.float32
+    anywhere = pl.BlockSpec(memory_space=pl.ANY)
+    dma = pltpu.SemaphoreType.DMA
+    return pl.pallas_call(
+        fused_kernel,
+        out_shape=jax.ShapeDtypeStruct((tokens, columns), bf16),
+        in_specs=[anywhere] * 8,
+        out_specs=pl.BlockSpec(memory_space=pltpu.VMEM),
+        scratch_shapes=[
+            pltpu.VMEM((rows, model), bf16),
+            pltpu.VMEM((1, model), f32),
+            pltpu.VMEM((1, tokens), jnp.int32),
+            pltpu.VMEM((1, adapters), jnp.int32),
+            pltpu.VMEM(down_factor_weight.shape, bf16),
+            pltpu.VMEM(up_factor_weight.shape, bf16),
+            pltpu.VMEM((chunks, LINES, 2, 2, 16, half), bf16),
+            pltpu.VMEM((chunks, tokens, CHUNK), bf16),
+            pltpu.VMEM((slots, CHUNK, columns), bf16),
+            pltpu.VMEM((slots, CHUNK, columns), bf16),
+            pltpu.VMEM((tokens, columns), f32),
+            pltpu.VMEM((tokens, columns), f32),
+            pltpu.VMEM((tokens, 64), f32),
+            pltpu.VMEM((members, 16, 128), bf16),
+            dma((4,)),
+            dma,
+            dma,
+            dma((slots,)),
+            dma((slots,)),
+            dma((chunks, LINES)),
+            dma((chunks, LINES)),
+            dma((chunks,)),
+            dma((chunks,)),
+            dma((chunks,)),
+            dma((chunks,)),
+            dma((members,)),
+            dma((members,)),
+        ],
+        compiler_params=pltpu.CompilerParams(
+            collective_id=0, has_side_effects=True, vmem_limit_bytes=60 * 1024 * 1024
+        ),
+        cost_estimate=pl.CostEstimate(
+            flops=4 * tokens * model * columns,
+            bytes_accessed=4 * model * columns,
+            transcendentals=tokens * columns,
+        ),
+    )(
+        residual,
+        prenorm_scale.reshape(1, model),
+        gate_weight_matrix,
+        up_weight_matrix,
+        down_factor_weight,
+        up_factor_weight,
+        token_adapter_ids.reshape(1, tokens),
+        adapter_store_rows.reshape(1, adapters),
+    )
+
+
 def solution(mesh):
     in_specs = (
         P(("groups", "mp"), None),
@@ -81,6 +494,15 @@
         P(),
     )
     out_specs = P("groups", "mp")
+
+    def body(*args):
+        residual, _, gate, _, down, _, ids, store = args
+        rows, model = residual.shape
+        fits = supported(
+            mesh, model, gate.shape[1], store.shape[0], ids.shape[0], rows, down.shape[1]
+        )
+        return (fused if fits else on_device)(*args)
+
     return jax.shard_map(
-        on_device, mesh=mesh, in_specs=in_specs, out_specs=out_specs, check_vma=False
-    )
+        body, mesh=mesh, in_specs=in_specs, out_specs=out_specs, check_vma=False
+    )

time: 121 us -> 41.6 us (0.34)
  waiting for transfers between devices: 41.5 us -> 0 us
  Pallas kernels: 0 us -> 39.6 us
  matrix products: 34.1 us -> 0 us
  blocking collectives: 19.3 us -> 0 us
  between operations: 13.5 us -> 0.01 us
  local copies, waits for them, and re-layouts: 8.05 us -> 1.82 us
  other arithmetic: 4.05 us -> 0 us
    all_gather x1 -> x0, waiting for transfers between devices: 41.5 us -> none  [on_device(): gathered = lax.all_gather(normalized_input, 'mp', axis=0, tiled=True)]
    pallas_call x0 -> x1, Pallas kernels: none -> 39.6 us  [fused(): pl.pallas_call(fused_kernel, out_shape=jax.ShapeDtypeStruct((tokens, colu...]
    dot_general x4 -> x0, matrix products: 34.1 us -> none  [the longest x1 14.7 us: on_device(): jnp.dot(gathered, gate_weight_matrix, preferred_element_type=jnp.float32)]
    all_gather x1 -> x0, blocking collectives: 19.3 us -> none  [on_device(): lax.all_gather(flat_shrunk, 'mp', axis=0, tiled=True)]
    gather x3 -> x0, local copies, waits for them, and re-layouts: 6.32 us -> none  [the longest x1 2.84 us: on_device(): adapter_correction[0][store_row_index]]
    convert_element_type x2 -> x0, other arithmetic: 1.75 us -> none  [the longest x1 1.66 us: on_device(): normalized_input = (widened * rescale * prenorm_scale).astype(jnp.bfloat16)]
    unnamed x9 -> x1, local copies, waits for them, and re-layouts: 0.11 us -> 1.82 us
    squeeze x1 -> x0, local copies, waits for them, and re-layouts: 1.48 us -> none  [on_device(): adapter_correction[0][store_row_index]]
  transfers between devices with their start and end apart: 1 -> 0, of which waited for: 1 -> 0; matrix products, arithmetic and copies ran while one was open for 2% -> 0% of each run, Pallas kernels for 0% -> 0%
where the time goes in v1:
time: 41.6 us; the launch traced here: 41.5 us
  Pallas kernels  39.6 us (95%)
  local copies, waits for them, and re-layouts  1.82 us (4%)
    pallas_call x1, Pallas kernels, fused(): pl.pallas_call(fused_kernel, out_shape=jax.ShapeDtypeStruct((tokens, colu...  39.6 us
    unnamed x1, local copies, waits for them, and re-layouts  1.82 us

profile of v1, /device:TPU:0, one launch (start us, length us, event | category | flops | bytes accessed | tf_op | source)
XLA Modules:
  0.0 41.5 jit_solution(5286671549943608374)
XLA Ops:
  0.0 39.6 %shard_map.82 = bf16[128,1792]{1,0:T(8,128)(2,1)} custom-call(bf16[8,8192]{1,0:T(8,128)(2,1)} %residual_hbm.1, f32[1,8192]{1,0:T(1,128)} %bitcast.3, bf16[8192,1792]{1,0:T(8,128)(2,1)} %gate_hbm.1, bf16[8192,1792]{1,0:T(8,128)(2,1)} %up_hbm.1, bf16[2,32,8192]{2,1,0:T(8,128)(2,1)} %down_hbm.1, bf16[32,32,1792]{2,1,0:T(8,128)(2,1)} %factor_hbm.1, ...), custom_call_target="tpu_custom_call" | custom-call | flops 7516192768 | bytes 58720256 | tf_op jit(solution)/shard_map/pallas_call | solution.py:431
  39.7 1.8 %copy.10 = bf16[128,1792]{1,0:T(8,128)(2,1)} copy(bf16[128,1792]{1,0:T(8,128)(2,1)} %shard_map.82) | data formatting | bytes 917504

commit v2 on v1

--- a/solution.py
+++ b/solution.py
@@ -7,6 +7,9 @@
 
 SEGMENT_SLOTS = 8
 CHUNK = 1024
+CORE_LAG = 2
+USE_LAG = 3
+AHEAD = 4
 WIDE = 256
 LINES = 4
 LANES = 4
@@ -84,7 +87,7 @@
         and tokens == 128
         and rows == 8
         and model % CHUNK == 0
-        and model // CHUNK >= 4
+        and model // CHUNK >= 8
         and columns % 256 == 0
         and columns <= 2048
         and adapters == 2 * members
@@ -192,15 +195,15 @@
         second = slice(i * CHUNK + half, (i + 1) * CHUNK)
         top = residual[:, first].astype(f32) * rescale * scale[:, first]
         bottom = residual[:, second].astype(f32) * rescale * scale[:, second]
-        blocks[i, z, x, c] = jnp.concatenate([top, bottom], axis=0).astype(bf16)
+        blocks[i, x, c, z] = jnp.concatenate([top, bottom], axis=0).astype(bf16)
 
     pl.semaphore_wait(barrier, members - 1)
 
     def z_copy(i, k):
         other = lax.rem(z + k, LINES)
         return pltpu.make_async_remote_copy(
-            src_ref=blocks.at[i, z, x, c],
-            dst_ref=blocks.at[i, z, x, c],
+            src_ref=blocks.at[i, x, c, z],
+            dst_ref=blocks.at[i, x, c, z],
             send_sem=z_send.at[i, other],
             recv_sem=z_recv.at[i, z],
             device_id={"mp": other * LANES + x * 2 + c},
@@ -210,8 +213,8 @@
     def z_arrival(i, k):
         other = lax.rem(z + k, LINES)
         return pltpu.make_async_remote_copy(
-            src_ref=blocks.at[i, other, x, c],
-            dst_ref=blocks.at[i, other, x, c],
+            src_ref=blocks.at[i, x, c, other],
+            dst_ref=blocks.at[i, x, c, other],
             send_sem=z_send.at[i, other],
             recv_sem=z_recv.at[i, other],
             device_id={"mp": other * LANES + x * 2 + c},
@@ -220,8 +223,8 @@
 
     def x_copy(i, lane):
         return pltpu.make_async_remote_copy(
-            src_ref=blocks.at[i, :, lane, c],
-            dst_ref=blocks.at[i, :, lane, c],
+            src_ref=blocks.at[i, lane, c],
+            dst_ref=blocks.at[i, lane, c],
             send_sem=x_send.at[i],
             recv_sem=x_recv.at[i],
             device_id={"mp": z * LANES + (1 - x) * 2 + c},
@@ -230,8 +233,8 @@
 
     def c_copy(i, core):
         return pltpu.make_async_remote_copy(
-            src_ref=blocks.at[i, :, :, core],
-            dst_ref=blocks.at[i, :, :, core],
+            src_ref=blocks.at[i, :, core],
+            dst_ref=blocks.at[i, :, core],
             send_sem=c_send.at[i],
             recv_sem=c_recv.at[i],
             device_id={"mp": z * LANES + x * 2 + (1 - c)},
@@ -260,7 +263,7 @@
             device_id_type=MESH,
         )
 
-    @pl.loop(0, chunks)
+    @pl.loop(0, AHEAD)
     def _(i):
         for k in range(1, LINES):
             z_copy(i, k).start()
@@ -284,22 +287,28 @@
     slot_row = jnp.sum(in_slot * (earlier + SEGMENT_SLOTS * slot_number), axis=0, keepdims=True)
 
     def gather_step(g):
+        @pl.when(g + AHEAD < chunks)
+        def _():
+            for k in range(1, LINES):
+                z_copy(g + AHEAD, k).start()
+
         @pl.when(g < chunks)
         def _():
             for k in range(1, LINES):
                 z_arrival(g, k).wait_recv()
             x_copy(g, x).start()
 
-        @pl.when((g >= 1) & (g <= chunks))
+        @pl.when((g >= CORE_LAG) & (g < chunks + CORE_LAG))
         def _():
-            x_copy(g - 1, 1 - x).wait_recv()
-            c_copy(g - 1, c).start()
-
-        @pl.when((g >= 2) & (g <= chunks + 1))
+            x_copy(g - CORE_LAG, 1 - x).wait_recv()
+            c_copy(g - CORE_LAG, c).start()
+
+        @pl.when((g >= USE_LAG) & (g < chunks + USE_LAG))
         def _():
-            i = g - 2
+            i = g - USE_LAG
             c_copy(i, 1 - c).wait_recv()
-            taken = blocks[i].reshape(members, 16, half).astype(f32)
+            places = [(a, b, d) for d in range(LINES) for a in range(2) for b in range(2)]
+            taken = jnp.stack([blocks[i, a, b, d] for a, b, d in places]).astype(f32)
             for h in range(2):
                 part = taken[:, h * 8 : (h + 1) * 8, :].reshape(tokens, half).astype(bf16)
                 features[i, :, h * half : (h + 1) * half] = part
@@ -331,18 +340,15 @@
         def _():
             up_copy(i + slots).start()
 
-    for g in range(3):
+    @pl.loop(0, USE_LAG + 1)
+    def _(g):
         gather_step(g)
 
-    @pl.loop(0, chunks - 3)
+    @pl.loop(0, chunks - 1)
     def _(i):
         gate_step(i)
-        gather_step(3 + i + (i + 1) // 2)
+        gather_step(USE_LAG + 1 + i)
         up_step(i)
-
-        @pl.when(i % 2 == 0)
-        def _():
-            gather_step(4 + i + (i + 1) // 2)
 
     wanted = (me * 16 + lax.broadcasted_iota(jnp.int32, (16, tokens), 0)).astype(f32)
     chooser = (slot_row == wanted).astype(f32).astype(bf16)
@@ -357,10 +363,8 @@
     def _(k):
         s_copy(k).start()
 
-    @pl.loop(chunks - 3, chunks - 1)
-    def _(i):
-        gate_step(i)
-        up_step(i)
+    gate_step(chunks - 1)
+    up_step(chunks - 1)
 
     @pl.loop(1, members)
     def _(k):
@@ -388,8 +392,6 @@
             lambda cut, p=p: factor[:, p * 16 : (p + 1) * 16, cut].reshape(adapters * 16, WIDE),
         )
 
-    gate_step(chunks - 1)
-    up_step(chunks - 1)
     for j in range(columns // WIDE):
         cut = slice(j * WIDE, (j + 1) * WIDE)
         value = gate_total[:, cut]
@@ -440,7 +442,7 @@
             pltpu.VMEM((1, adapters), jnp.int32),
             pltpu.VMEM(down_factor_weight.shape, bf16),
             pltpu.VMEM(up_factor_weight.shape, bf16),
-            pltpu.VMEM((chunks, LINES, 2, 2, 16, half), bf16),
+            pltpu.VMEM((chunks, 2, 2, LINES, 16, half), bf16),
             pltpu.VMEM((chunks, tokens, CHUNK), bf16),
             pltpu.VMEM((slots, CHUNK, columns), bf16),
             pltpu.VMEM((slots, CHUNK, columns), bf16),

time: 41.6 us -> 38.2 us (0.918)
  Pallas kernels: 39.6 us -> 36.2 us
    pallas_call x1, Pallas kernels: 39.6 us -> 36.2 us  [fused(): pl.pallas_call(fused_kernel, out_shape=jax.ShapeDtypeStruct((tokens, colu...]
where the time goes in v2:
time: 38.2 us; the launch traced here: 38.1 us
  Pallas kernels  36.2 us (95%)
  local copies, waits for them, and re-layouts  1.82 us (5%)
    pallas_call x1, Pallas kernels, fused(): pl.pallas_call(fused_kernel, out_shape=jax.ShapeDtypeStruct((tokens, colu...  36.2 us
    unnamed x1, local copies, waits for them, and re-layouts  1.82 us

profile of v2, /device:TPU:0, one launch (start us, length us, event | category | flops | bytes accessed | tf_op | source)
XLA Modules:
  0.0 38.1 jit_solution(10359626643228105968)
XLA Ops:
  0.0 36.2 %shard_map.82 = bf16[128,1792]{1,0:T(8,128)(2,1)} custom-call(bf16[8,8192]{1,0:T(8,128)(2,1)} %residual_hbm.1, f32[1,8192]{1,0:T(1,128)} %bitcast.3, bf16[8192,1792]{1,0:T(8,128)(2,1)} %gate_hbm.1, bf16[8192,1792]{1,0:T(8,128)(2,1)} %up_hbm.1, bf16[2,32,8192]{2,1,0:T(8,128)(2,1)} %down_hbm.1, bf16[32,32,1792]{2,1,0:T(8,128)(2,1)} %factor_hbm.1, ...), custom_call_target="tpu_custom_call" | custom-call | flops 7516192768 | bytes 58720256 | tf_op jit(solution)/shard_map/pallas_call | solution.py:433
  36.3 1.8 %copy.10 = bf16[128,1792]{1,0:T(8,128)(2,1)} copy(bf16[128,1792]{1,0:T(8,128)(2,1)} %shard_map.82) | data formatting | bytes 917504
